TPU v7x, 512 devices: a whole 4x8x8 slice. The times are simulated.
512 devices in a mesh: row: 16 (over z, core), col: 32 (over x, y).
Axes of the slice: x: 4, y: 8, z: 8, core: 2. Of those that a mesh axis runs over, the one named last changes fastest.
Arguments:
- front: float32 [12288, 12288], P('row', 'col'), as said below
- structure: int32 [3, 96], replicated, may hold values from 0 to 1, as said below
- factor_front: float32 [3, 12288, 512], P(None, 'row', 'col'), may hold values from -0.0546875 to 0.0546875
- factor_border: float32 [2, 512, 512], replicated, may hold values from -0.6 to 0.6
- pivot_inverse: float32 [3, 512, 512], P(None, 'row')
Outputs:
- inverse_front: float32 [3, 512, 12288], P(None, 'row', 'col')
- inverse_parent: float32 [2, 512, 512], P(None, 'row')
- inverse_diagonal: float32 [3, 512, 512], P(None, 'row')
Inputs may be any that keep to these rules, and one draw needn't show every extreme that they name: front is exactly symmetric. structure[k, b] = 1 where front block b (rows b * 128 to (b + 1) * 128 - 1) lies in supernode k's structure; every 1 in row k is also a 1 in row k - 1; blocks b < 24 are 1 in every row.
All inputs are finite; a program needn't handle non-finite values.
Results may differ from a plain program's by a relative error of at most 0.0001.
Values sent between devices are 32-bit elements; how exact they have to be, the bound alone decides.
A program may use at most 64 MiB of HBM per device.

v0:
```python
import jax
import jax.numpy as jnp
from jax import lax
from jax.sharding import Mesh
from jax.sharding import PartitionSpec as P

BLK = 128
ROW = ("row_0", "row_1")
HIGH = lax.Precision.HIGHEST


def broadcast_by_axis(x, axes, root):
    x = jnp.where(lax.axis_index(axes) == root, x, jnp.zeros_like(x))
    for axis in axes:
        x = lax.psum(x, axis)
    return x


def split_up(x, dim, length):
    dims = x.shape
    pieces = x.reshape(*dims[:dim], length, dims[dim] // length, *dims[dim + 1 :])
    return jnp.moveaxis(pieces, dim, 0)


def sent_and_summed(x, axis, dim):
    length = lax.axis_size(axis)
    pieces = lax.all_to_all(split_up(x, dim, length), axis, 0, 0, tiled=True)
    return jnp.sum(pieces, axis=0)


def padded_to(lines, length):
    spare = -lines.shape[0] % length
    if not spare:
        return lines
    return jnp.concatenate([lines, jnp.zeros((spare, *lines.shape[1:]), lines.dtype)])


def in_order(pieces, dim):
    pieces = jnp.moveaxis(pieces, 0, dim)
    dims = pieces.shape
    return pieces.reshape(*dims[:dim], dims[dim] * dims[dim + 1], *dims[dim + 2 :])


def from_everyone(x, axis):
    copies = jnp.broadcast_to(x, (lax.axis_size(axis), *x.shape))
    return lax.all_to_all(copies, axis, split_axis=0, concat_axis=0, tiled=True)


def collect(x, axis, dim):
    return in_order(from_everyone(x, axis), dim)


def total_of(x, axes):
    lines = x.reshape(-1, x.shape[-1])
    own = sent_and_summed(padded_to(lines, lax.axis_size(axes)), axes, 0)
    whole = collect(own, axes, 0)
    return whole[: len(lines)].reshape(x.shape)


def matmul(former, latter):
    return jnp.dot(former, latter, precision=HIGH, preferred_element_type=jnp.float32)


def contract_first(former, latter):
    return lax.dot_general(
        former, latter, (((0,), (0,)), ((), ())), precision=HIGH, preferred_element_type=jnp.float32
    )


def block_flags(structure_row, first_row, rows_count):
    position = first_row + jnp.arange(rows_count, dtype=jnp.int32)
    owners = position // BLK
    numbers = jnp.arange(structure_row.shape[0], dtype=jnp.int32)
    matches = (owners[:, None] == numbers[None, :]).astype(jnp.float32)
    return jnp.dot(matches, structure_row.astype(jnp.float32), precision=HIGH)


def body(front, structure, factor_front, factor_border, pivot_inverse):
    row_index = lax.axis_index(ROW)
    col_index = lax.axis_index("col")
    rows_here = front.shape[0]
    cols_here = front.shape[1]
    width_here = pivot_inverse.shape[1]
    supers = structure.shape[0]
    row_first = row_index * rows_here
    col_first = col_index * cols_here
    fetched = lax.all_gather(factor_front, "col", axis=2, tiled=True)
    fronts = []
    parents = []
    diagonals = []
    previous = None
    diag_prev = None
    for section in range(supers):
        gathered = fetched[section]
        row_flags = block_flags(structure[section], row_first, rows_here)
        factor_rows = gathered * row_flags[:, None]
        own_half = lax.dynamic_slice_in_dim(factor_rows, col_index % 2 * cols_here, cols_here, 0)
        factor_cols = broadcast_by_axis(own_half, ROW, col_index // 2)
        partial_value = contract_first(factor_rows, front)
        if section > 0:
            border = factor_border[section - 1]
            border_rows = lax.dynamic_slice_in_dim(border, row_index * width_here, width_here, 0)
            partial_value = partial_value + contract_first(border_rows, previous)
            parent_part = total_of(matmul(previous, factor_cols), "col")
            parent_rows = parent_part + matmul(diag_prev, border)
            parent_all = lax.all_gather(parent_rows, ROW, axis=0, tiled=True)
            parents.append(-parent_rows)
        image_rows = sent_and_summed(partial_value, ROW, 0)
        col_flags = block_flags(structure[section], col_first, cols_here)
        current = -(image_rows * col_flags[None, :])
        gram_rows = total_of(matmul(image_rows, factor_cols), "col")
        diag_now = pivot_inverse[section] + gram_rows
        if section > 0:
            parent_slice = lax.dynamic_slice_in_dim(
                parent_all, row_index * width_here, width_here, 1
            )
            diag_now = diag_now + contract_first(parent_slice, border)
        fronts.append(current)
        diagonals.append(diag_now)
        previous = current
        diag_prev = diag_now
    return (jnp.stack(fronts), jnp.stack(parents), jnp.stack(diagonals))


def solution(mesh):
    torus = Mesh(mesh.devices.reshape(8, 2, mesh.shape["col"]), ("row_0", "row_1", "col"))
    return jax.shard_map(
        body,
        mesh=torus,
        in_specs=(P(ROW, "col"), P(), P(None, ROW, "col"), P(), P(None, ROW, None)),
        out_specs=(P(None, ROW, "col"), P(None, ROW, None), P(None, ROW, None)),
        check_vma=False,
    )
```

profile of v0, /device:TPU:1, one launch (start us, length us, event | category | flops | bytes accessed | tf_op | source)
XLA Modules:
  0.0 465.4 jit_solution(13938320989205049159)
XLA Ops:
  11.3 91.5 %all-gather.4.cloned.1.call-done = f32[3,768,512]{1,2,0:T(8,128)} async-done(((f32[3,768,16]{1,2,0:T(8,128)}), f32[3,768,512]{1,2,0:T(8,128)}) %all-gather.4.cloned.1.call-update) | async-done | bytes 4718608 | tf_op jit(solution)/shard_map/all_gather | solution.py:87
  102.8 2.8 fusion
  106.6 1.4 dynamic-slice_select_fusion
  108.1 87.4 %all-reduce.5.cloned.1.call-done = (f32[384,512]{0,1:T(8,128)}, f32[384,512]{0,1:T(8,128)}, f32[384,512]{0,1:T(8,128)}) async-done(((f32[384,512]{0,1:T(8,128)}, f32[384,512]{0,1:T(8,128)}, f32[384,512]{0,1:T(8,128)}), (f32[384,512]{0,1:T(8,128)}, f32[384,512]{0,1:T(8,128)}, f32[384,512]{0,1:T(8,128)})) %all-reduce.5.cloned.1.call-update) | async-done | bytes 2359312 | tf_op jit(solution)/shard_map/psum | solution.py:15
  195.5 3.6 fusion.3
  199.1 8.3 %all-to-all-start = ((f32[16,32,384]{2,1,0:T(8,128)}), f32[16,32,384]{2,1,0:T(8,128)}, u32[]{:S(2)}, u32[]{:S(2)}) async-start(f32[16,32,384]{2,1,0:T(8,128)} %fusion.3), calls=%async_computation | async-start | bytes 1572864 | tf_op jit(solution)/shard_map/all_to_all | solution.py:27
  207.8 22.4 %all-to-all-done = f32[16,32,384]{2,1,0:T(8,128)} async-done(((f32[16,32,384]{2,1,0:T(8,128)}), f32[16,32,384]{2,1,0:T(8,128)}, u32[]{:S(2)}, u32[]{:S(2)}) %all-to-all-start) | async-done | bytes 786464 | tf_op jit(solution)/shard_map/all_to_all | solution.py:27
  231.4 8.4 %all-reduce.7.cloned.1.call-done = (f32[384,512]{0,1:T(8,128)}, f32[384,512]{0,1:T(8,128)}, f32[384,512]{0,1:T(8,128)}) async-done(((f32[384,512]{0,1:T(8,128)}, f32[384,512]{0,1:T(8,128)}, f32[384,512]{0,1:T(8,128)}), (f32[384,512]{0,1:T(8,128)}, f32[384,512]{0,1:T(8,128)}, f32[384,512]{0,1:T(8,128)})) %all-reduce.7.cloned.1.call-update) | async-done | bytes 2359312 | tf_op jit(solution)/shard_map/psum | solution.py:15
  239.8 2.0 convolution_bitcast_fusion.3
  242.5 8.3 %all-to-all-start.5 = ((f32[32,1,512]{2,1,0:T(1,128)}), f32[32,1,512]{2,1,0:T(1,128)S(1)}, u32[]{:S(2)}, u32[]{:S(2)}) async-start(f32[32,1,512]{2,1,0:T(1,128)} %copy.9), calls=%async_computation.5 | async-start | bytes 131072 | tf_op jit(solution)/shard_map/all_to_all | solution.py:27
  250.8 2.0 convolution_bitcast_fusion.4
  253.4 6.2 %all-to-all-done.5 = f32[32,1,512]{2,1,0:T(1,128)S(1)} async-done(((f32[32,1,512]{2,1,0:T(1,128)}), f32[32,1,512]{2,1,0:T(1,128)S(1)}, u32[]{:S(2)}, u32[]{:S(2)}) %all-to-all-start.5) | async-done | bytes 65568 | tf_op jit(solution)/shard_map/all_to_all | solution.py:27
  259.6 3.9 all-to-all-start.3
  263.5 1.5 fusion.64
  265.1 7.3 %all-to-all-done.3 = f32[32,1,512]{2,1,0:T(1,128)S(1)} async-done(((f32[32,1,512]{2,1,0:T(1,128)}), f32[32,1,512]{2,1,0:T(1,128)S(1)}, u32[]{:S(2)}, u32[]{:S(2)}) %all-to-all-start.3) | async-done | bytes 65568 | tf_op jit(solution)/shard_map/all_to_all | solution.py:27
  273.0 3.9 all-to-all-start.6
  276.9 2.6 fusion.21
  279.5 6.2 %all-to-all-done.6 = f32[32,1,512]{2,1,0:T(1,128)S(1)} async-done(((f32[32,1,512]{2,1,0:T(1,128)}), f32[32,1,512]{2,1,0:T(1,128)S(1)}, u32[]{:S(2)}, u32[]{:S(2)}) %all-to-all-start.6) | async-done | bytes 65568 | tf_op jit(solution)/shard_map/all_to_all | solution.py:46
  286.4 3.9 all-to-all-start.4
  290.3 5.1 %convolution_add_fusion.1 = f32[512,384]{1,0:T(8,128)} fusion(f32[512,384]{1,0:T(8,128)} %fusion.21, f32[768,512]{0,1:T(8,128)} %copy-done.3, f32[768,384]{1,0:T(8,128)S(1)} %copy-done), kind=kOutput, calls=%fused_computation.7 | convolution fusion | flops 1812135936 | bytes 4325376 | tf_op jit(solution)/shard_map/dot_general | solution.py:65
  295.4 3.7 all-to-all-done.4
  299.1 12.6 %all-to-all-start.1 = ((f32[16,32,384]{2,1,0:T(8,128)}), f32[16,32,384]{2,1,0:T(8,128)}, u32[]{:S(2)}, u32[]{:S(2)}) async-start(f32[16,32,384]{2,1,0:T(8,128)} %bitcast.123), calls=%async_computation.1 | async-start | bytes 1572864 | tf_op jit(solution)/shard_map/all_to_all | solution.py:27
  312.8 2.2 convolution_add_fusion.3
  315.4 19.6 %all-to-all-done.1 = f32[16,32,384]{2,1,0:T(8,128)} async-done(((f32[16,32,384]{2,1,0:T(8,128)}), f32[16,32,384]{2,1,0:T(8,128)}, u32[]{:S(2)}, u32[]{:S(2)}) %all-to-all-start.1) | async-done | bytes 786464 | tf_op jit(solution)/shard_map/all_to_all | solution.py:27
  335.0 1.2 reduce_sum.80
  336.2 2.0 convolution_bitcast_fusion.2
  338.9 4.1 all-to-all-start.7
  343.0 2.0 convolution_bitcast_fusion.1
  345.7 6.2 %all-to-all-done.7 = f32[32,1,512]{2,1,0:T(1,128)S(1)} async-done(((f32[32,1,512]{2,1,0:T(1,128)}), f32[32,1,512]{2,1,0:T(1,128)S(1)}, u32[]{:S(2)}, u32[]{:S(2)}) %all-to-all-start.7) | async-done | bytes 65568 | tf_op jit(solution)/shard_map/all_to_all | solution.py:27
  352.5 3.9 all-to-all-start.9
  357.3 8.5 %all-to-all-done.9 = f32[32,1,512]{2,1,0:T(1,128)S(1)} async-done(((f32[32,1,512]{2,1,0:T(1,128)}), f32[32,1,512]{2,1,0:T(1,128)S(1)}, u32[]{:S(2)}, u32[]{:S(2)}) %all-to-all-start.9) | async-done | bytes 65568 | tf_op jit(solution)/shard_map/all_to_all | solution.py:27
  366.4 3.9 all-to-all-start.8
  370.3 2.6 fusion.19
  373.8 5.4 %all-to-all-done.8 = f32[32,1,512]{2,1,0:T(1,128)S(1)} async-done(((f32[32,1,512]{2,1,0:T(1,128)}), f32[32,1,512]{2,1,0:T(1,128)S(1)}, u32[]{:S(2)}, u32[]{:S(2)}) %all-to-all-start.8) | async-done | bytes 65568 | tf_op jit(solution)/shard_map/all_to_all | solution.py:46
  379.9 4.6 all-to-all-start.10
  384.4 5.1 %convolution_add_fusion = f32[512,384]{1,0:T(8,128)} fusion(f32[512,384]{1,0:T(8,128)} %fusion.19, f32[768,512]{0,1:T(8,128)} %copy-done.2, f32[768,384]{1,0:T(8,128)S(1)} %copy-done), kind=kOutput, calls=%fused_computation.6 | convolution fusion | flops 1812135936 | bytes 4325376 | tf_op jit(solution)/shard_map/dot_general | solution.py:65
  389.6 3.8 all-to-all-done.10
  393.4 7.4 %all-to-all-start.2 = ((f32[16,32,384]{2,1,0:T(8,128)}), f32[16,32,384]{2,1,0:T(8,128)}, u32[]{:S(2)}, u32[]{:S(2)}) async-start(f32[16,32,384]{2,1,0:T(8,128)} %bitcast.122), calls=%async_computation.2 | async-start | bytes 1572864 | tf_op jit(solution)/shard_map/all_to_all | solution.py:27
  400.9 1.7 convolution_add_fusion.5
  403.2 1.3 convolution_add_fusion.2
  406.8 17.4 %all-to-all-done.2 = f32[16,32,384]{2,1,0:T(8,128)} async-done(((f32[16,32,384]{2,1,0:T(8,128)}), f32[16,32,384]{2,1,0:T(8,128)}, u32[]{:S(2)}, u32[]{:S(2)}) %all-to-all-start.2) | async-done | bytes 786464 | tf_op jit(solution)/shard_map/all_to_all | solution.py:27
  425.3 2.0 convolution_bitcast_fusion
  428.0 4.6 all-to-all-start.11
  432.6 1.5 pad_maximum_fusion.1
  434.1 7.3 %all-to-all-done.11 = f32[32,1,512]{2,1,0:T(1,128)} async-done(((f32[32,1,512]{2,1,0:T(1,128)}), f32[32,1,512]{2,1,0:T(1,128)}, u32[]{:S(2)}, u32[]{:S(2)}) %all-to-all-start.11) | async-done | bytes 65568 | tf_op jit(solution)/shard_map/all_to_all | solution.py:27
  442.9 4.5 all-to-all-start.12
  449.0 7.4 %all-to-all-done.12 = f32[32,1,512]{2,1,0:T(1,128)} async-done(((f32[32,1,512]{2,1,0:T(1,128)}), f32[32,1,512]{2,1,0:T(1,128)}, u32[]{:S(2)}, u32[]{:S(2)}) %all-to-all-start.12) | async-done | bytes 65568 | tf_op jit(solution)/shard_map/all_to_all | solution.py:46
  456.4 1.7 fusion.5
  (70 shorter events, 24.6 us)
Async XLA Ops:
  7.2 188.4 %copy-start = (f32[768,384]{1,0:T(8,128)S(1)}, f32[768,384]{1,0:T(8,128)}, u32[]{:S(2)}) copy-start(f32[768,384]{1,0:T(8,128)} %param.5) | copy-start | bytes 3538948
  7.2 95.6 %all-gather.4.cloned.1.call-start = ((), (), s32[]{:S(2)}) async-start(), calls=%async_computation.13 | async-start | bytes 4866048 | tf_op jit(solution)/shard_map/all_gather | solution.py:87
  7.9 187.6 %all-reduce.5.cloned.1.call-start = ((), (), s32[]{:S(2)}) async-start(), calls=%async_computation.16 | async-start | bytes 4718592 | tf_op jit(solution)/shard_map/psum | solution.py:15
  105.6 2.4 copy-start.2
  105.6 2.4 copy-start.3
  108.0 131.8 %all-reduce.7.cloned.1.call-start = ((), (), s32[]{:S(2)}) async-start(), calls=%async_computation.17 | async-start | bytes 4718592 | tf_op jit(solution)/shard_map/psum | solution.py:15
  199.1 8.3 %copy-start.11 = (s32[3,96]{1,0:T(4,128)S(1)}, s32[3,96]{1,0:T(4,128)}, u32[]{:S(2)}) copy-start(s32[3,96]{1,0:T(4,128)} %param.6) | copy-start | bytes 3460
  199.1 31.1 %all-to-all-start = ((f32[16,32,384]{2,1,0:T(8,128)}), f32[16,32,384]{2,1,0:T(8,128)}, u32[]{:S(2)}, u32[]{:S(2)}) async-start(f32[16,32,384]{2,1,0:T(8,128)} %fusion.3), calls=%async_computation | async-start | bytes 1572864 | tf_op jit(solution)/shard_map/all_to_all | solution.py:27
  207.8 55.7 %copy-start.1 = (f32[2,512,512]{2,1,0:T(8,128)S(1)}, f32[2,512,512]{2,1,0:T(8,128)}, u32[]{:S(2)}) copy-start(f32[2,512,512]{2,1,0:T(8,128)} %param.8) | copy-start | bytes 6291460
  242.5 17.1 %all-to-all-start.5 = ((f32[32,1,512]{2,1,0:T(1,128)}), f32[32,1,512]{2,1,0:T(1,128)S(1)}, u32[]{:S(2)}, u32[]{:S(2)}) async-start(f32[32,1,512]{2,1,0:T(1,128)} %copy.9), calls=%async_computation.5 | async-start | bytes 131072 | tf_op jit(solution)/shard_map/all_to_all | solution.py:27
  259.6 12.7 %all-to-all-start.3 = ((f32[32,1,512]{2,1,0:T(1,128)}), f32[32,1,512]{2,1,0:T(1,128)S(1)}, u32[]{:S(2)}, u32[]{:S(2)}) async-start(f32[32,1,512]{2,1,0:T(1,128)} %copy.8), calls=%async_computation.3 | async-start | bytes 131072 | tf_op jit(solution)/shard_map/all_to_all | solution.py:27
  273.0 12.7 %all-to-all-start.6 = ((f32[32,1,512]{2,1,0:T(1,128)}), f32[32,1,512]{2,1,0:T(1,128)S(1)}, u32[]{:S(2)}, u32[]{:S(2)}) async-start(f32[32,1,512]{2,1,0:T(1,128)} %broadcast_in_dim.11), calls=%async_computation.6 | async-start | bytes 131072 | tf_op jit(solution)/shard_map/all_to_all | solution.py:46
  286.4 12.7 %all-to-all-start.4 = ((f32[32,1,512]{2,1,0:T(1,128)}), f32[32,1,512]{2,1,0:T(1,128)S(1)}, u32[]{:S(2)}, u32[]{:S(2)}) async-start(f32[32,1,512]{2,1,0:T(1,128)} %broadcast_in_dim.10), calls=%async_computation.4 | async-start | bytes 131072 | tf_op jit(solution)/shard_map/all_to_all | solution.py:46
  299.1 12.6 %copy-start.7 = (f32[32,1,512]{2,1,0:T(1,128)}, f32[32,1,512]{2,1,0:T(1,128)S(1)}, u32[]{:S(2)}) copy-start(f32[32,1,512]{2,1,0:T(1,128)S(1)} %all-to-all-done.4) | copy-start | bytes 196612
  299.1 35.9 %all-to-all-start.1 = ((f32[16,32,384]{2,1,0:T(8,128)}), f32[16,32,384]{2,1,0:T(8,128)}, u32[]{:S(2)}, u32[]{:S(2)}) async-start(f32[16,32,384]{2,1,0:T(8,128)} %bitcast.123), calls=%async_computation.1 | async-start | bytes 1572864 | tf_op jit(solution)/shard_map/all_to_all | solution.py:27
  311.7 89.1 %all-gather.6.cloned.1.call-start = ((), (), s32[]{:S(2)}) async-start(), calls=%async_computation.14 | async-start | bytes 1114112 | tf_op jit(solution)/shard_map/all_gather | solution.py:106
  338.9 13.0 %all-to-all-start.7 = ((f32[32,1,512]{2,1,0:T(1,128)}), f32[32,1,512]{2,1,0:T(1,128)S(1)}, u32[]{:S(2)}, u32[]{:S(2)}) async-start(f32[32,1,512]{2,1,0:T(1,128)} %copy.10), calls=%async_computation.7 | async-start | bytes 131072 | tf_op jit(solution)/shard_map/all_to_all | solution.py:27
  351.9 0.6 copy-start.9
  352.5 13.3 %all-to-all-start.9 = ((f32[32,1,512]{2,1,0:T(1,128)}), f32[32,1,512]{2,1,0:T(1,128)S(1)}, u32[]{:S(2)}, u32[]{:S(2)}) async-start(f32[32,1,512]{2,1,0:T(1,128)} %copy.11), calls=%async_computation.9 | async-start | bytes 131072 | tf_op jit(solution)/shard_map/all_to_all | solution.py:27
  365.8 0.7 copy-start.8
  366.4 12.7 %all-to-all-start.8 = ((f32[32,1,512]{2,1,0:T(1,128)}), f32[32,1,512]{2,1,0:T(1,128)S(1)}, u32[]{:S(2)}, u32[]{:S(2)}) async-start(f32[32,1,512]{2,1,0:T(1,128)} %broadcast_in_dim.12), calls=%async_computation.8 | async-start | bytes 131072 | tf_op jit(solution)/shard_map/all_to_all | solution.py:46
  379.9 13.5 %all-to-all-start.10 = ((f32[32,1,512]{2,1,0:T(1,128)}), f32[32,1,512]{2,1,0:T(1,128)}, u32[]{:S(2)}, u32[]{:S(2)}) async-start(f32[32,1,512]{2,1,0:T(1,128)} %broadcast_in_dim.13), calls=%async_computation.10 | async-start | bytes 131072 | tf_op jit(solution)/shard_map/all_to_all | solution.py:46
  393.4 30.7 %all-to-all-start.2 = ((f32[16,32,384]{2,1,0:T(8,128)}), f32[16,32,384]{2,1,0:T(8,128)}, u32[]{:S(2)}, u32[]{:S(2)}) async-start(f32[16,32,384]{2,1,0:T(8,128)} %bitcast.122), calls=%async_computation.2 | async-start | bytes 1572864 | tf_op jit(solution)/shard_map/all_to_all | solution.py:27
  400.8 55.6 %all-gather.8.cloned.1.call-start = ((), (), s32[]{:S(2)}) async-start(), calls=%async_computation.15 | async-start | bytes 1114112 | tf_op jit(solution)/shard_map/all_gather | solution.py:106
  402.6 0.6 copy-start.5
  404.6 42.9 %copy-start.4 = (f32[32,512]{1,0:T(8,128)S(1)}, f32[32,512]{1,0:T(8,128)}, u32[]{:S(2)}) copy-start(f32[32,512]{1,0:T(8,128)} %convolution_add_fusion.3) | copy-start | bytes 196612
  406.7 25.8 %copy-start.10 = (f32[384]{0:T(512)S(1)}, f32[384]{0:T(512)}, u32[]{:S(2)}) copy-start(f32[384]{0:T(512)} %convolution_reduce_fusion.3) | copy-start | bytes 4612
  427.3 30.9 %copy-start.6 = (f32[32,512]{1,0:T(8,128)S(1)}, f32[32,512]{1,0:T(8,128)}, u32[]{:S(2)}) copy-start(f32[32,512]{1,0:T(8,128)} %copy-done.5) | copy-start | bytes 196612
  428.0 13.4 %all-to-all-start.11 = ((f32[32,1,512]{2,1,0:T(1,128)}), f32[32,1,512]{2,1,0:T(1,128)}, u32[]{:S(2)}, u32[]{:S(2)}) async-start(f32[32,1,512]{2,1,0:T(1,128)} %copy.12), calls=%async_computation.11 | async-start | bytes 131072 | tf_op jit(solution)/shard_map/all_to_all | solution.py:27
  442.9 13.5 %all-to-all-start.12 = ((f32[32,1,512]{2,1,0:T(1,128)}), f32[32,1,512]{2,1,0:T(1,128)}, u32[]{:S(2)}, u32[]{:S(2)}) async-start(f32[32,1,512]{2,1,0:T(1,128)} %broadcast_in_dim.14), calls=%async_computation.12 | async-start | bytes 131072 | tf_op jit(solution)/shard_map/all_to_all | solution.py:46
Sparse Core Ops, SparseCore 0:
  11.2 91.5 all-gather.3
  108.1 87.3 all-reduce.4
  198.6 41.2 all-reduce.6
  315.2 39.2 all-gather.5
  404.7 38.7 all-gather.7
where the time goes:
time: 467 us; the launch traced here: 465 us
  waiting for transfers between devices  310 us (66%)
  starting transfers between devices  74.1 us (16%)
  matrix products  40.5 us (9%)
  other arithmetic  17.4 us (4%)
  between operations  14.1 us (3%)
  local copies, waits for them, and re-layouts  9.62 us (2%)
    psum x2, waiting for transfers between devices, broadcast_by_axis(): x = lax.psum(x, axis)  95.9 us
    all_to_all x8, waiting for transfers between devices, sent_and_summed(): pieces = lax.all_to_all(split_up(x, dim, length), axis, 0, 0, tiled=True)  94.9 us
    all_gather x1, waiting for transfers between devices, body(): fetched = lax.all_gather(factor_front, 'col', axis=2, tiled=True)  91.5 us
    all_to_all x8, starting transfers between devices, sent_and_summed(): pieces = lax.all_to_all(split_up(x, dim, length), axis, 0, 0, tiled=True)  53 us
    all_to_all x5, waiting for transfers between devices, from_everyone(): return lax.all_to_all(copies, axis, split_axis=0, concat_axis=0, tiled=True)  26.6 us
    dot_general x7, matrix products, contract_first(): lax.dot_general(former, latter, (((0,), (0,)), ((), ())), precision=HIGH,...  22.4 us
    all_to_all x5, starting transfers between devices, from_everyone(): return lax.all_to_all(copies, axis, split_axis=0, concat_axis=0, tiled=True)  20.7 us
    dot_general x7, matrix products, matmul(): jnp.dot(former, latter, precision=HIGH, preferred_element_type=jnp.float32)  13.3 us
  transfers between devices with their start and end apart: 18, of which 16 were waited for; matrix products, arithmetic and copies ran while one was open for 12% of the time, Pallas kernels for 0%

commit v1 on v0

--- a/solution.py
+++ b/solution.py
@@ -84,7 +84,9 @@
     supers = structure.shape[0]
     row_first = row_index * rows_here
     col_first = col_index * cols_here
-    fetched = lax.all_gather(factor_front, "col", axis=2, tiled=True)
+    fetched = jnp.concatenate(
+        lax.all_to_all(jnp.stack([factor_front] * lax.axis_size("col")), "col", 0, 0), axis=2
+    )
     fronts = []
     parents = []
     diagonals = []

time: 467 us -> 498 us (1.066)
  waiting for transfers between devices: 310 us -> 325 us
  starting transfers between devices: 74.1 us -> 84.9 us
  local copies, waits for them, and re-layouts: 9.62 us -> 18.2 us
    all_to_all x0 -> x1, waiting for transfers between devices: none -> 103 us  [body(): lax.all_to_all(jnp.stack([factor_front] * lax.axis_size('col')), 'col', 0...]
    all_gather x1 -> x0, waiting for transfers between devices: 91.5 us -> none  [body(): fetched = lax.all_gather(factor_front, 'col', axis=2, tiled=True)]
    all_to_all x0 -> x1, starting transfers between devices: none -> 10.7 us  [body(): lax.all_to_all(jnp.stack([factor_front] * lax.axis_size('col')), 'col', 0...]
  transfers between devices with their start and end apart: 18 -> 18, of which waited for: 16 -> 16; matrix products, arithmetic and copies ran while one was open for 12% -> 11% of each run, Pallas kernels for 0% -> 0%
where the time goes in v1:
time: 498 us; the launch traced here: 496 us
  waiting for transfers between devices  325 us (65%)
  starting transfers between devices  84.9 us (17%)
  matrix products  38.5 us (8%)
  local copies, waits for them, and re-layouts  18.2 us (4%)
  other arithmetic  15.4 us (3%)
  between operations  14.2 us (3%)
    all_to_all x1, waiting for transfers between devices, body(): lax.all_to_all(jnp.stack([factor_front] * lax.axis_size('col')), 'col', 0...  103 us
    psum x2, waiting for transfers between devices, broadcast_by_axis(): x = lax.psum(x, axis)  101 us
    all_to_all x8, waiting for transfers between devices, sent_and_summed(): pieces = lax.all_to_all(split_up(x, dim, length), axis, 0, 0, tiled=True)  94.8 us
    all_to_all x8, starting transfers between devices, sent_and_summed(): pieces = lax.all_to_all(split_up(x, dim, length), axis, 0, 0, tiled=True)  52.9 us
    all_to_all x5, waiting for transfers between devices, from_everyone(): return lax.all_to_all(copies, axis, split_axis=0, concat_axis=0, tiled=True)  26.3 us
    dot_general x7, matrix products, contract_first(): lax.dot_general(former, latter, (((0,), (0,)), ((), ())), precision=HIGH,...  22.4 us
    all_to_all x5, starting transfers between devices, from_everyone(): return lax.all_to_all(copies, axis, split_axis=0, concat_axis=0, tiled=True)  20.9 us
    dot_general x7, matrix products, matmul(): jnp.dot(former, latter, precision=HIGH, preferred_element_type=jnp.float32)  13.3 us
  transfers between devices with their start and end apart: 18, of which 16 were waited for; matrix products, arithmetic and copies ran while one was open for 11% of the time, Pallas kernels for 0%

profile of v1, /device:TPU:1, one launch (start us, length us, event | category | flops | bytes accessed | tf_op | source)
XLA Modules:
  0.0 496.3 jit_solution(9563995603728379249)
XLA Ops:
  7.2 3.8 stack.16
  11.0 10.7 %all-to-all-start = ((f32[32,3,768,16]{2,3,1,0:T(8,128)}), f32[32,3,768,16]{2,3,1,0:T(8,128)}, u32[]{:S(2)}, u32[]{:S(2)}) async-start(f32[32,3,768,16]{2,3,1,0:T(8,128)} %stack.16), calls=%async_computation | async-start | bytes 9437184 | tf_op jit(solution)/shard_map/all_to_all | solution.py:88
  23.0 103.3 %all-to-all-done = f32[32,3,768,16]{2,3,1,0:T(8,128)} async-done(((f32[32,3,768,16]{2,3,1,0:T(8,128)}), f32[32,3,768,16]{2,3,1,0:T(8,128)}, u32[]{:S(2)}, u32[]{:S(2)}) %all-to-all-start) | async-done | bytes 4718624 | tf_op jit(solution)/shard_map/all_to_all | solution.py:88
  126.3 2.7 fusion.61
  134.4 92.2 %all-reduce.5.cloned.1.call-done = (f32[384,512]{0,1:T(8,128)}, f32[384,512]{0,1:T(8,128)}, f32[384,512]{0,1:T(8,128)}) async-done(((f32[384,512]{0,1:T(8,128)}, f32[384,512]{0,1:T(8,128)}, f32[384,512]{0,1:T(8,128)}), (f32[384,512]{0,1:T(8,128)}, f32[384,512]{0,1:T(8,128)}, f32[384,512]{0,1:T(8,128)})) %all-reduce.5.cloned.1.call-update) | async-done | bytes 2359312 | tf_op jit(solution)/shard_map/psum | solution.py:15
  226.7 3.6 fusion
  230.3 8.2 %all-to-all-start.1 = ((f32[16,32,384]{2,1,0:T(8,128)}), f32[16,32,384]{2,1,0:T(8,128)}, u32[]{:S(2)}, u32[]{:S(2)}) async-start(f32[16,32,384]{2,1,0:T(8,128)} %fusion), calls=%async_computation.1 | async-start | bytes 1572864 | tf_op jit(solution)/shard_map/all_to_all | solution.py:27
  238.8 22.4 %all-to-all-done.1 = f32[16,32,384]{2,1,0:T(8,128)} async-done(((f32[16,32,384]{2,1,0:T(8,128)}), f32[16,32,384]{2,1,0:T(8,128)}, u32[]{:S(2)}, u32[]{:S(2)}) %all-to-all-start.1) | async-done | bytes 786464 | tf_op jit(solution)/shard_map/all_to_all | solution.py:27
  262.4 8.5 %all-reduce.7.cloned.1.call-done = (f32[384,512]{0,1:T(8,128)}, f32[384,512]{0,1:T(8,128)}, f32[384,512]{0,1:T(8,128)}) async-done(((f32[384,512]{0,1:T(8,128)}, f32[384,512]{0,1:T(8,128)}, f32[384,512]{0,1:T(8,128)}), (f32[384,512]{0,1:T(8,128)}, f32[384,512]{0,1:T(8,128)}, f32[384,512]{0,1:T(8,128)})) %all-reduce.7.cloned.1.call-update) | async-done | bytes 2359312 | tf_op jit(solution)/shard_map/psum | solution.py:15
  270.9 2.0 convolution_bitcast_fusion.3
  273.6 8.3 %all-to-all-start.6 = ((f32[32,1,512]{2,1,0:T(1,128)}), f32[32,1,512]{2,1,0:T(1,128)S(1)}, u32[]{:S(2)}, u32[]{:S(2)}) async-start(f32[32,1,512]{2,1,0:T(1,128)} %copy.9), calls=%async_computation.6 | async-start | bytes 131072 | tf_op jit(solution)/shard_map/all_to_all | solution.py:27
  281.9 2.0 convolution_bitcast_fusion.4
  284.6 6.2 %all-to-all-done.6 = f32[32,1,512]{2,1,0:T(1,128)S(1)} async-done(((f32[32,1,512]{2,1,0:T(1,128)}), f32[32,1,512]{2,1,0:T(1,128)S(1)}, u32[]{:S(2)}, u32[]{:S(2)}) %all-to-all-start.6) | async-done | bytes 65568 | tf_op jit(solution)/shard_map/all_to_all | solution.py:27
  290.7 3.9 all-to-all-start.4
  294.6 1.5 fusion.62
  296.2 7.2 %all-to-all-done.4 = f32[32,1,512]{2,1,0:T(1,128)S(1)} async-done(((f32[32,1,512]{2,1,0:T(1,128)}), f32[32,1,512]{2,1,0:T(1,128)S(1)}, u32[]{:S(2)}, u32[]{:S(2)}) %all-to-all-start.4) | async-done | bytes 65568 | tf_op jit(solution)/shard_map/all_to_all | solution.py:27
  304.1 3.9 all-to-all-start.7
  308.0 2.6 fusion.18
  310.6 6.2 %all-to-all-done.7 = f32[32,1,512]{2,1,0:T(1,128)S(1)} async-done(((f32[32,1,512]{2,1,0:T(1,128)}), f32[32,1,512]{2,1,0:T(1,128)S(1)}, u32[]{:S(2)}, u32[]{:S(2)}) %all-to-all-start.7) | async-done | bytes 65568 | tf_op jit(solution)/shard_map/all_to_all | solution.py:46
  317.5 4.0 all-to-all-start.5
  321.6 5.1 %convolution_add_fusion.1 = f32[512,384]{1,0:T(8,128)} fusion(f32[512,384]{1,0:T(8,128)} %fusion.18, f32[768,512]{0,1:T(8,128)} %copy-done.3, f32[768,384]{1,0:T(8,128)S(1)} %copy-done), kind=kOutput, calls=%fused_computation.4 | convolution fusion | flops 1812135936 | bytes 4325376 | tf_op jit(solution)/shard_map/dot_general | solution.py:65
  326.7 3.6 all-to-all-done.5
  330.2 12.6 %all-to-all-start.2 = ((f32[16,32,384]{2,1,0:T(8,128)}), f32[16,32,384]{2,1,0:T(8,128)}, u32[]{:S(2)}, u32[]{:S(2)}) async-start(f32[16,32,384]{2,1,0:T(8,128)} %bitcast.118), calls=%async_computation.2 | async-start | bytes 1572864 | tf_op jit(solution)/shard_map/all_to_all | solution.py:27
  343.8 2.2 convolution_add_fusion.3
  346.3 19.9 %all-to-all-done.2 = f32[16,32,384]{2,1,0:T(8,128)} async-done(((f32[16,32,384]{2,1,0:T(8,128)}), f32[16,32,384]{2,1,0:T(8,128)}, u32[]{:S(2)}, u32[]{:S(2)}) %all-to-all-start.2) | async-done | bytes 786464 | tf_op jit(solution)/shard_map/all_to_all | solution.py:27
  367.3 2.0 convolution_bitcast_fusion.2
  370.0 4.1 all-to-all-start.8
  374.1 2.0 convolution_bitcast_fusion.1
  376.8 6.2 %all-to-all-done.8 = f32[32,1,512]{2,1,0:T(1,128)S(1)} async-done(((f32[32,1,512]{2,1,0:T(1,128)}), f32[32,1,512]{2,1,0:T(1,128)S(1)}, u32[]{:S(2)}, u32[]{:S(2)}) %all-to-all-start.8) | async-done | bytes 65568 | tf_op jit(solution)/shard_map/all_to_all | solution.py:27
  383.6 3.9 all-to-all-start.10
  388.4 8.5 %all-to-all-done.10 = f32[32,1,512]{2,1,0:T(1,128)S(1)} async-done(((f32[32,1,512]{2,1,0:T(1,128)}), f32[32,1,512]{2,1,0:T(1,128)S(1)}, u32[]{:S(2)}, u32[]{:S(2)}) %all-to-all-start.10) | async-done | bytes 65568 | tf_op jit(solution)/shard_map/all_to_all | solution.py:27
  397.6 3.9 all-to-all-start.9
  401.4 2.6 fusion.16
  404.9 5.4 %all-to-all-done.9 = f32[32,1,512]{2,1,0:T(1,128)S(1)} async-done(((f32[32,1,512]{2,1,0:T(1,128)}), f32[32,1,512]{2,1,0:T(1,128)S(1)}, u32[]{:S(2)}, u32[]{:S(2)}) %all-to-all-start.9) | async-done | bytes 65568 | tf_op jit(solution)/shard_map/all_to_all | solution.py:46
  411.0 4.6 all-to-all-start.11
  415.5 5.1 %convolution_add_fusion = f32[512,384]{1,0:T(8,128)} fusion(f32[512,384]{1,0:T(8,128)} %fusion.16, f32[768,512]{0,1:T(8,128)} %copy-done.2, f32[768,384]{1,0:T(8,128)S(1)} %copy-done), kind=kOutput, calls=%fused_computation.3 | convolution fusion | flops 1812135936 | bytes 4325376 | tf_op jit(solution)/shard_map/dot_general | solution.py:65
  420.7 3.8 all-to-all-done.11
  424.5 7.5 %all-to-all-start.3 = ((f32[16,32,384]{2,1,0:T(8,128)}), f32[16,32,384]{2,1,0:T(8,128)}, u32[]{:S(2)}, u32[]{:S(2)}) async-start(f32[16,32,384]{2,1,0:T(8,128)} %bitcast.117), calls=%async_computation.3 | async-start | bytes 1572864 | tf_op jit(solution)/shard_map/all_to_all | solution.py:27
  432.2 1.7 convolution_add_fusion.5
  434.6 1.3 convolution_add_fusion.2
  438.1 17.0 %all-to-all-done.3 = f32[16,32,384]{2,1,0:T(8,128)} async-done(((f32[16,32,384]{2,1,0:T(8,128)}), f32[16,32,384]{2,1,0:T(8,128)}, u32[]{:S(2)}, u32[]{:S(2)}) %all-to-all-start.3) | async-done | bytes 786464 | tf_op jit(solution)/shard_map/all_to_all | solution.py:27
  456.3 2.0 convolution_bitcast_fusion
  459.0 4.6 all-to-all-start.12
  463.6 1.5 pad_maximum_fusion.1
  465.0 7.3 %all-to-all-done.12 = f32[32,1,512]{2,1,0:T(1,128)} async-done(((f32[32,1,512]{2,1,0:T(1,128)}), f32[32,1,512]{2,1,0:T(1,128)}, u32[]{:S(2)}, u32[]{:S(2)}) %all-to-all-start.12) | async-done | bytes 65568 | tf_op jit(solution)/shard_map/all_to_all | solution.py:27
  473.9 4.6 all-to-all-start.13
  480.0 7.3 %all-to-all-done.13 = f32[32,1,512]{2,1,0:T(1,128)} async-done(((f32[32,1,512]{2,1,0:T(1,128)}), f32[32,1,512]{2,1,0:T(1,128)}, u32[]{:S(2)}, u32[]{:S(2)}) %all-to-all-start.13) | async-done | bytes 65568 | tf_op jit(solution)/shard_map/all_to_all | solution.py:46
  487.3 1.7 fusion.2
  (74 shorter events, 27.3 us)
Async XLA Ops:
  7.2 219.5 %copy-start = (f32[768,384]{1,0:T(8,128)S(1)}, f32[768,384]{1,0:T(8,128)}, u32[]{:S(2)}) copy-start(f32[768,384]{1,0:T(8,128)} %param.5) | copy-start | bytes 3538948
  11.0 10.9 %copy-start.11 = (s32[3,96]{1,0:T(4,128)S(1)}, s32[3,96]{1,0:T(4,128)}, u32[]{:S(2)}) copy-start(s32[3,96]{1,0:T(4,128)} %param.6) | copy-start | bytes 3460
  11.0 115.3 %all-to-all-start = ((f32[32,3,768,16]{2,3,1,0:T(8,128)}), f32[32,3,768,16]{2,3,1,0:T(8,128)}, u32[]{:S(2)}, u32[]{:S(2)}) async-start(f32[32,3,768,16]{2,3,1,0:T(8,128)} %stack.16), calls=%async_computation | async-start | bytes 9437184 | tf_op jit(solution)/shard_map/all_to_all | solution.py:88
  21.7 204.9 %all-reduce.5.cloned.1.call-start = ((), (), s32[]{:S(2)}) async-start(), calls=%async_computation.16 | async-start | bytes 4718592 | tf_op jit(solution)/shard_map/psum | solution.py:15
  129.1 1.2 copy-start.2
  132.2 1.1 copy-start.3
  134.4 136.6 %all-reduce.7.cloned.1.call-start = ((), (), s32[]{:S(2)}) async-start(), calls=%async_computation.17 | async-start | bytes 4718592 | tf_op jit(solution)/shard_map/psum | solution.py:15
  230.3 31.0 %all-to-all-start.1 = ((f32[16,32,384]{2,1,0:T(8,128)}), f32[16,32,384]{2,1,0:T(8,128)}, u32[]{:S(2)}, u32[]{:S(2)}) async-start(f32[16,32,384]{2,1,0:T(8,128)} %fusion), calls=%async_computation.1 | async-start | bytes 1572864 | tf_op jit(solution)/shard_map/all_to_all | solution.py:27
  238.8 55.8 %copy-start.1 = (f32[2,512,512]{2,1,0:T(8,128)S(1)}, f32[2,512,512]{2,1,0:T(8,128)}, u32[]{:S(2)}) copy-start(f32[2,512,512]{2,1,0:T(8,128)} %param.8) | copy-start | bytes 6291460
  273.6 17.1 %all-to-all-start.6 = ((f32[32,1,512]{2,1,0:T(1,128)}), f32[32,1,512]{2,1,0:T(1,128)S(1)}, u32[]{:S(2)}, u32[]{:S(2)}) async-start(f32[32,1,512]{2,1,0:T(1,128)} %copy.9), calls=%async_computation.6 | async-start | bytes 131072 | tf_op jit(solution)/shard_map/all_to_all | solution.py:27
  290.7 12.7 %all-to-all-start.4 = ((f32[32,1,512]{2,1,0:T(1,128)}), f32[32,1,512]{2,1,0:T(1,128)S(1)}, u32[]{:S(2)}, u32[]{:S(2)}) async-start(f32[32,1,512]{2,1,0:T(1,128)} %copy.8), calls=%async_computation.4 | async-start | bytes 131072 | tf_op jit(solution)/shard_map/all_to_all | solution.py:27
  304.1 12.7 %all-to-all-start.7 = ((f32[32,1,512]{2,1,0:T(1,128)}), f32[32,1,512]{2,1,0:T(1,128)S(1)}, u32[]{:S(2)}, u32[]{:S(2)}) async-start(f32[32,1,512]{2,1,0:T(1,128)} %broadcast_in_dim.11), calls=%async_computation.7 | async-start | bytes 131072 | tf_op jit(solution)/shard_map/all_to_all | solution.py:46
  317.5 12.7 %all-to-all-start.5 = ((f32[32,1,512]{2,1,0:T(1,128)}), f32[32,1,512]{2,1,0:T(1,128)S(1)}, u32[]{:S(2)}, u32[]{:S(2)}) async-start(f32[32,1,512]{2,1,0:T(1,128)} %broadcast_in_dim.10), calls=%async_computation.5 | async-start | bytes 131072 | tf_op jit(solution)/shard_map/all_to_all | solution.py:46
  330.2 12.6 %copy-start.7 = (f32[32,1,512]{2,1,0:T(1,128)}, f32[32,1,512]{2,1,0:T(1,128)S(1)}, u32[]{:S(2)}) copy-start(f32[32,1,512]{2,1,0:T(1,128)S(1)} %all-to-all-done.5) | copy-start | bytes 196612
  330.2 35.9 %all-to-all-start.2 = ((f32[16,32,384]{2,1,0:T(8,128)}), f32[16,32,384]{2,1,0:T(8,128)}, u32[]{:S(2)}, u32[]{:S(2)}) async-start(f32[16,32,384]{2,1,0:T(8,128)} %bitcast.118), calls=%async_computation.2 | async-start | bytes 1572864 | tf_op jit(solution)/shard_map/all_to_all | solution.py:27
  342.9 89.4 %all-gather.3.cloned.1.call-start = ((), (), s32[]{:S(2)}) async-start(), calls=%async_computation.14 | async-start | bytes 1114112 | tf_op jit(solution)/shard_map/all_gather | solution.py:108
  370.0 13.0 %all-to-all-start.8 = ((f32[32,1,512]{2,1,0:T(1,128)}), f32[32,1,512]{2,1,0:T(1,128)S(1)}, u32[]{:S(2)}, u32[]{:S(2)}) async-start(f32[32,1,512]{2,1,0:T(1,128)} %copy.10), calls=%async_computation.8 | async-start | bytes 131072 | tf_op jit(solution)/shard_map/all_to_all | solution.py:27
  383.0 0.6 copy-start.9
  383.6 13.3 %all-to-all-start.10 = ((f32[32,1,512]{2,1,0:T(1,128)}), f32[32,1,512]{2,1,0:T(1,128)S(1)}, u32[]{:S(2)}, u32[]{:S(2)}) async-start(f32[32,1,512]{2,1,0:T(1,128)} %copy.11), calls=%async_computation.10 | async-start | bytes 131072 | tf_op jit(solution)/shard_map/all_to_all | solution.py:27
  396.9 0.7 copy-start.8
  397.6 12.7 %all-to-all-start.9 = ((f32[32,1,512]{2,1,0:T(1,128)}), f32[32,1,512]{2,1,0:T(1,128)S(1)}, u32[]{:S(2)}, u32[]{:S(2)}) async-start(f32[32,1,512]{2,1,0:T(1,128)} %broadcast_in_dim.12), calls=%async_computation.9 | async-start | bytes 131072 | tf_op jit(solution)/shard_map/all_to_all | solution.py:46
  411.0 13.5 %all-to-all-start.11 = ((f32[32,1,512]{2,1,0:T(1,128)}), f32[32,1,512]{2,1,0:T(1,128)}, u32[]{:S(2)}, u32[]{:S(2)}) async-start(f32[32,1,512]{2,1,0:T(1,128)} %broadcast_in_dim.13), calls=%async_computation.11 | async-start | bytes 131072 | tf_op jit(solution)/shard_map/all_to_all | solution.py:46
  424.5 30.6 %all-to-all-start.3 = ((f32[16,32,384]{2,1,0:T(8,128)}), f32[16,32,384]{2,1,0:T(8,128)}, u32[]{:S(2)}, u32[]{:S(2)}) async-start(f32[16,32,384]{2,1,0:T(8,128)} %bitcast.117), calls=%async_computation.3 | async-start | bytes 1572864 | tf_op jit(solution)/shard_map/all_to_all | solution.py:27
  431.9 55.4 %all-gather.5.cloned.1.call-start = ((), (), s32[]{:S(2)}) async-start(), calls=%async_computation.15 | async-start | bytes 1114112 | tf_op jit(solution)/shard_map/all_gather | solution.py:108
  434.0 0.6 copy-start.5
  435.9 42.6 %copy-start.4 = (f32[32,512]{1,0:T(8,128)S(1)}, f32[32,512]{1,0:T(8,128)}, u32[]{:S(2)}) copy-start(f32[32,512]{1,0:T(8,128)} %convolution_add_fusion.3) | copy-start | bytes 196612
  438.1 25.4 %copy-start.10 = (f32[384]{0:T(512)S(1)}, f32[384]{0:T(512)}, u32[]{:S(2)}) copy-start(f32[384]{0:T(512)} %convolution_reduce_fusion.3) | copy-start | bytes 4612
  458.2 30.8 %copy-start.6 = (f32[32,512]{1,0:T(8,128)S(1)}, f32[32,512]{1,0:T(8,128)}, u32[]{:S(2)}) copy-start(f32[32,512]{1,0:T(8,128)} %copy-done.5) | copy-start | bytes 196612
  459.0 13.4 %all-to-all-start.12 = ((f32[32,1,512]{2,1,0:T(1,128)}), f32[32,1,512]{2,1,0:T(1,128)}, u32[]{:S(2)}, u32[]{:S(2)}) async-start(f32[32,1,512]{2,1,0:T(1,128)} %copy.12), calls=%async_computation.12 | async-start | bytes 131072 | tf_op jit(solution)/shard_map/all_to_all | solution.py:27
  473.9 13.4 %all-to-all-start.13 = ((f32[32,1,512]{2,1,0:T(1,128)}), f32[32,1,512]{2,1,0:T(1,128)}, u32[]{:S(2)}, u32[]{:S(2)}) async-start(f32[32,1,512]{2,1,0:T(1,128)} %broadcast_in_dim.14), calls=%async_computation.13 | async-start | bytes 131072 | tf_op jit(solution)/shard_map/all_to_all | solution.py:46
Sparse Core Ops, SparseCore 0:
  134.5 92.1 all-reduce.4
  229.7 41.2 all-reduce.6
  346.6 38.9 all-gather.2
  436.1 38.5 all-gather.4
